TPU v7x, 32 devices: a whole 2x2x4 slice. The times are simulated.
32 devices in a mesh: row: 8 (over z, core), col: 4 (over y, x).
Axes of the slice: x: 2, y: 2, z: 4, core: 2. Of those that a mesh axis runs over, the one named last changes fastest.
Arguments:
- chars: bfloat16 [512, 8192], P(('row', 'col')), may hold values from -6 to 6
- pool_weight: bfloat16 [32768, 8192], P('col', 'row'), may hold values from -0.5 to 0.5
- gain_attn: bfloat16 [8192], P('row'), may hold values from 0.099609375 to 1.8984375
- w_query: bfloat16 [8192, 8192], P('row', 'col'), may hold values from -0.5 to 0.5
- w_key: bfloat16 [8192, 8192], P('row', 'col'), may hold values from -3 to 3
- w_value: bfloat16 [8192, 8192], P('row', 'col'), may hold values from -0.0625 to 0.0625
- w_out: bfloat16 [8192, 8192], P('col', 'row'), may hold values from -0.0625 to 0.0625
- gain_ffn: bfloat16 [8192], P('row'), may hold values from 0.099609375 to 1.8984375
- w_gate: bfloat16 [8192, 28672], P('row', 'col'), may hold values from -0.0625 to 0.0625
- w_up: bfloat16 [8192, 28672], P('row', 'col'), may hold values from -0.0625 to 0.0625
- w_down: bfloat16 [28672, 8192], P('col', 'row'), may hold values from -0.03125 to 0.03125
Outputs:
- upsampled: bfloat16 [512, 8192], P(('row', 'col'))
All inputs are finite; a program needn't handle non-finite values.
Results may differ from a plain program's by a relative error of at most 0.02.
Values may be sent and summed in bfloat16 or wider, within the bound.
A program may use at most 256 MiB of HBM per device.

v0:
```python
import jax
import jax.numpy as jnp
from jax import lax
from jax.sharding import PartitionSpec as P

D = 8192
HD = 128
POOL = 4


EPS = 1e-05


def square_sum(hidden):
    values = hidden.astype(jnp.float32)
    return jnp.sum(values * values, axis=-1)


def norm_apply(hidden, totals, gain):
    factor = lax.rsqrt(totals / D + EPS)[..., None]
    return (hidden.astype(jnp.float32) * factor * gain.astype(jnp.float32)).astype(jnp.bfloat16)


def attend(queries, keys_part, values_part, offset):
    query_count = queries.shape[0]
    key_count = keys_part.shape[0]
    query_heads = queries.reshape(query_count, -1, HD)
    key_heads = keys_part.reshape(key_count, -1, HD)
    value_heads = values_part.reshape(key_count, -1, HD)
    scores = jnp.einsum(
        "qhd,khd->hqk", query_heads, key_heads, preferred_element_type=jnp.float32
    ) * HD ** (-0.5)
    query_places = offset + jnp.arange(query_count, dtype=jnp.int32)
    key_places = jnp.arange(key_count, dtype=jnp.int32)
    allowed = query_places[:, None] >= key_places[None, :]
    scores = jnp.where(allowed[None], scores, jnp.float32(-1e30))
    highest = jnp.max(scores, axis=-1, keepdims=True)
    weights = jnp.exp(scores - highest)
    weights = (weights / jnp.sum(weights, axis=-1, keepdims=True)).astype(jnp.bfloat16)
    mixed = jnp.einsum("hqk,khd->qhd", weights, value_heads, preferred_element_type=jnp.float32)
    return mixed.astype(jnp.bfloat16).reshape(query_count, -1)


def on_device(
    chars, pool_weight, gain_attn, w_query, w_key, w_value, w_out, gain_ffn, w_gate, w_up, w_down
):
    rows_count = lax.axis_size("row")
    cols_count = lax.axis_size("col")
    char_rows = chars.shape[0]
    tokens_here = char_rows // POOL
    feature_block = pool_weight.shape[1]
    grouped = chars.reshape(1, 1, tokens_here, POOL * chars.shape[1])
    spread = lax.all_to_all(grouped, "col", split_axis=3, concat_axis=1, tiled=True)
    piece = lax.all_gather(spread, "row", axis=0, tiled=True)
    pool_terms = jnp.dot(
        piece.reshape(-1, piece.shape[3]), pool_weight, preferred_element_type=jnp.float32
    )
    pool_terms = pool_terms.reshape(rows_count, cols_count, tokens_here, feature_block)
    pooled = lax.psum_scatter(
        pool_terms.astype(jnp.bfloat16), "col", scatter_dimension=1, tiled=True
    )
    attn_totals = lax.psum(square_sum(pooled), "row")
    normed_attn = norm_apply(pooled, attn_totals, gain_attn)
    gathered = lax.all_gather(normed_attn, "col", axis=1, tiled=True).reshape(-1, feature_block)
    seq_length = gathered.shape[0]
    block_rows = seq_length // rows_count
    slab = gathered
    queries = lax.psum_scatter(
        jnp.dot(slab, w_query, preferred_element_type=jnp.float32).astype(jnp.bfloat16),
        "row",
        scatter_dimension=0,
        tiled=True,
    )
    slab = gathered
    pair_local = lax.psum_scatter(
        jnp.concatenate(
            [
                jnp.dot(slab, w_key, preferred_element_type=jnp.float32),
                jnp.dot(slab, w_value, preferred_element_type=jnp.float32),
            ],
            axis=1,
        ).astype(jnp.bfloat16),
        "row",
        scatter_dimension=0,
        tiled=True,
    )
    pair_whole = lax.all_gather(pair_local, "row", axis=0, tiled=True)
    head_columns = w_query.shape[1]
    keys_part = pair_whole[:, :head_columns]
    values_part = pair_whole[:, head_columns:]
    mixed = attend(queries, keys_part, values_part, lax.axis_index("row") * block_rows)
    out_terms = jnp.dot(
        lax.all_gather(mixed, "row", axis=0, tiled=True), w_out, preferred_element_type=jnp.float32
    )
    out_terms = out_terms.reshape(rows_count, cols_count, tokens_here, feature_block)
    attn_total = lax.psum_scatter(
        out_terms.astype(jnp.bfloat16), "col", scatter_dimension=1, tiled=True
    ).astype(jnp.float32)
    first = (pooled.astype(jnp.float32) + attn_total).astype(jnp.bfloat16)
    ffn_totals = lax.psum(square_sum(first), "row")
    normed_ffn = norm_apply(first, ffn_totals, gain_ffn)
    gathered_ffn = lax.all_gather(normed_ffn, "col", axis=1, tiled=True).reshape(-1, feature_block)
    hidden_local = w_gate.shape[1]
    slab = gathered_ffn
    hidden_pair = lax.psum_scatter(
        jnp.concatenate(
            [
                jnp.dot(slab, w_gate, preferred_element_type=jnp.float32),
                jnp.dot(slab, w_up, preferred_element_type=jnp.float32),
            ],
            axis=1,
        ).astype(jnp.bfloat16),
        "row",
        scatter_dimension=0,
        tiled=True,
    ).astype(jnp.float32)
    activated = (jax.nn.silu(hidden_pair[:, :hidden_local]) * hidden_pair[:, hidden_local:]).astype(
        jnp.bfloat16
    )
    down_terms = jnp.dot(
        lax.all_gather(activated, "row", axis=0, tiled=True),
        w_down,
        preferred_element_type=jnp.float32,
    )
    down_terms = down_terms.reshape(rows_count, cols_count, tokens_here, feature_block)
    ffn_total = lax.psum_scatter(
        down_terms.astype(jnp.bfloat16), "col", scatter_dimension=1, tiled=True
    ).astype(jnp.float32)
    second = (first.astype(jnp.float32) + ffn_total).astype(jnp.bfloat16)
    returned = lax.all_to_all(second, "row", split_axis=0, concat_axis=3, tiled=True)
    expanded = jnp.repeat(returned.reshape(tokens_here, -1), POOL, axis=0)
    return (chars.astype(jnp.float32) + expanded.astype(jnp.float32)).astype(jnp.bfloat16)


def solution(mesh):
    return jax.shard_map(
        on_device,
        mesh=mesh,
        in_specs=(
            P(("row", "col"), None),
            P("col", "row"),
            P("row"),
            P("row", "col"),
            P("row", "col"),
            P("row", "col"),
            P("col", "row"),
            P("row"),
            P("row", "col"),
            P("row", "col"),
            P("col", "row"),
        ),
        out_specs=P(("row", "col"), None),
        check_vma=False,
    )
```

profile of v0, /device:TPU:0, one launch (start us, length us, event | category | flops | bytes accessed | tf_op | source)
XLA Modules:
  0.0 683.1 jit_solution(8492887767687466561)
XLA Ops:
  6.5 1.2 reshape.76
  7.8 25.5 %copy.36 = bf16[1,1,4,32768]{2,1,0,3:T(2,128)(2,1)} copy(bf16[1,1,4,32768]{3,2,1,0:T(4,128)(2,1)S(1)} %reshape.76) | data formatting | bytes 524288 | tf_op jit(solution)/shard_map/reshape | solution.py:52
  33.3 0.5 broadcast.39
  33.8 179.1 %reduce.2 = bf16[32768,4]{1,0:T(8,128)(2,1)} reduce(bf16[32768,1,1,4]{3,2,1,0:T(2,128)(2,1)} %bitcast.67, bf16[]{:T(256)} %broadcast.39), dimensions={1,2}, to_apply=%bitcast.45.reduce_sub_computation | reduce | bytes 524290
  212.9 18.1 %reshape.90 = bf16[4,2,16384]{2,1,0:T(2,128)(2,1)S(1)} reshape(bf16[32768,4]{1,0:T(8,128)(2,1)} %reduce.2) | data formatting | bytes 524288
  231.0 10.7 %all_to_all.27 = bf16[4,2,16384]{2,1,0:T(2,128)(2,1)S(1)} all-to-all(bf16[4,2,16384]{2,1,0:T(2,128)(2,1)S(1)} %reshape.90), channel_id=1, replica_groups=mesh['row'=8,'col'=4] {'col'}, dimensions={0} | all-to-all | bytes 524288 | tf_op jit(solution)/shard_map/all_to_all | solution.py:53
  241.7 21.1 %reshape.91 = bf16[32768,1,1,4]{3,2,1,0:T(2,128)(2,1)} reshape(bf16[4,2,16384]{2,1,0:T(2,128)(2,1)S(1)} %all_to_all.27) | data formatting | bytes 524288
  262.8 30.6 %copy.37 = bf16[1,1,4,32768]{3,2,1,0:T(4,128)(2,1)S(1)} copy(bf16[1,1,4,32768]{2,1,0,3:T(2,128)(2,1)} %bitcast.68) | data formatting | bytes 524288 | tf_op jit(solution)/shard_map/all_to_all | solution.py:53
  293.6 0.9 copy.38
  294.6 28.9 %all-gather.9.cloned.1.call-done = bf16[8,4,1,4,8192]{4,3,2,1,0:T(4,128)(2,1)} async-done(((bf16[1,4,1,4,8192]{4,3,2,1,0:T(4,128)(2,1)}), bf16[8,4,1,4,8192]{4,3,2,1,0:T(4,128)(2,1)}) %all-gather.9.cloned.1.call-update) | async-done | bytes 2097168 | tf_op jit(solution)/shard_map/all_gather | solution.py:54
  323.5 10.4 %fusion.5 = bf16[8,4,4,1024]{3,0,2,1:T(8,128)(2,1)} fusion(bf16[8192,1024]{1,0:T(8,128)(2,1)} %param.12, bf16[8,4,1,4,8192]{4,3,2,1,0:T(4,128)(2,1)} %all-gather.9.cloned.1.call-done), kind=kOutput, calls=%fused_computation.12 | convolution fusion | flops 2147614720 | bytes 19136512 | tf_op jit(solution)/shard_map/dot_general | solution.py:55
  334.0 23.6 %reduce-scatter.19.cloned.1.call-done = bf16[8,1,4,1024]{3,0,2,1:T(8,128)(2,1)} async-done(((bf16[8,4,4,1024]{3,0,2,1:T(8,128)(2,1)}), bf16[8,1,4,1024]{3,0,2,1:T(8,128)(2,1)}) %reduce-scatter.19.cloned.1.call-update) | async-done | bytes 65552
  357.6 0.9 fusion.19
  358.6 15.9 %psum.14 = f32[8,1,4]{0,2,1:T(4,128)S(1)} all-reduce(f32[8,1,4]{0,2,1:T(4,128)S(1)} %bitcast.73), channel_id=1, replica_groups=mesh['row'=8,'col'=4] {'row'}, use_global_device_ids=true, to_apply=%region_2.0 | all-reduce | flops 32 | bytes 256 | tf_op jit(solution)/shard_map/psum | solution.py:62
  374.5 0.9 fusion.21
  375.4 9.1 %all_gather.19 = bf16[8,4,4,1024]{3,0,2,1:T(8,128)(2,1)S(1)} all-gather(bf16[8,1,4,1024]{3,0,2,1:T(8,128)(2,1)S(1)} %fusion.21), channel_id=1, replica_groups=mesh['row'=8,'col'=4] {'col'}, dimensions={1}, use_global_device_ids=true | all-gather | bytes 327680 | tf_op jit(solution)/shard_map/all_gather | solution.py:64
  384.8 3.1 convolution_convert_fusion.3
  387.8 0.4 copy-done
  388.2 0.7 convolution_convert_fusion.4
  388.9 1.1 pad_maximum_fusion.1
  390.1 29.6 %reduce-scatter.13.cloned.1.call-done = bf16[16,4096]{1,0:T(8,128)(2,1)} async-done(((bf16[128,4096]{1,0:T(8,128)(2,1)}), bf16[16,4096]{1,0:T(8,128)(2,1)}) %reduce-scatter.13.cloned.1.call-update) | async-done | bytes 131088 | tf_op jit(solution)/shard_map/reduce_scatter | solution.py:75
  419.8 3.7 convolution_convert_fusion.2
  423.6 18.1 %all-gather.5.cloned.1.call-done = bf16[128,4096]{1,0:T(8,128)(2,1)} async-done(((bf16[16,4096]{1,0:T(8,128)(2,1)}), bf16[128,4096]{1,0:T(8,128)(2,1)}) %all-gather.5.cloned.1.call-update) | async-done | bytes 1048592 | tf_op jit(solution)/shard_map/all_gather | solution.py:87
  441.7 1.3 slice_bitcast_fusion.1
  443.0 31.5 %reduce-scatter.15.cloned.1.call-done = bf16[16,2048]{1,0:T(8,128)(2,1)} async-done(((bf16[128,2048]{1,0:T(8,128)(2,1)}), bf16[16,2048]{1,0:T(8,128)(2,1)}) %reduce-scatter.15.cloned.1.call-update) | async-done | bytes 65552 | tf_op jit(solution)/shard_map/reduce_scatter | solution.py:68
  474.5 1.2 fusion.11
  476.0 0.5 fusion.13
  476.5 15.0 %all_gather.21 = bf16[128,2048]{1,0:T(8,128)(2,1)S(1)} all-gather(bf16[16,2048]{1,0:T(8,128)(2,1)S(1)} %bitcast.71), channel_id=1, replica_groups=mesh['row'=8,'col'=4] {'row'}, dimensions={0}, use_global_device_ids=true | all-gather | bytes 589824 | tf_op jit(solution)/shard_map/all_gather | solution.py:93
  491.5 2.9 convolution_convert_fusion.5
  494.6 0.9 copy.45
  495.5 22.4 %reduce-scatter.21.cloned.1.call-done = bf16[8,1,4,1024]{3,0,2,1:T(8,128)(2,1)} async-done(((bf16[8,4,4,1024]{3,0,2,1:T(8,128)(2,1)}), bf16[8,1,4,1024]{3,0,2,1:T(8,128)(2,1)}) %reduce-scatter.21.cloned.1.call-update) | async-done | bytes 65552
  517.9 0.9 fusion.23
  518.9 15.9 %psum.15 = f32[8,1,4]{0,2,1:T(4,128)S(1)} all-reduce(f32[8,1,4]{0,2,1:T(4,128)S(1)} %bitcast.72), channel_id=1, replica_groups=mesh['row'=8,'col'=4] {'row'}, use_global_device_ids=true, to_apply=%region_9.10 | all-reduce | flops 32 | bytes 256 | tf_op jit(solution)/shard_map/psum | solution.py:100
  534.8 0.9 fusion.25
  535.7 9.3 %all_gather.22 = bf16[8,4,4,1024]{3,0,2,1:T(8,128)(2,1)S(1)} all-gather(bf16[8,1,4,1024]{3,0,2,1:T(8,128)(2,1)S(1)} %fusion.25), channel_id=1, replica_groups=mesh['row'=8,'col'=4] {'col'}, dimensions={1}, use_global_device_ids=true | all-gather | bytes 327680 | tf_op jit(solution)/shard_map/all_gather | solution.py:102
  545.3 7.3 %convolution_convert_fusion = bf16[128,7168]{1,0:T(8,128)(2,1)S(1)} fusion(bf16[128,1024]{1,0:T(8,128)(2,1)S(1)} %reshape.82, bf16[1024,7168]{1,0:T(8,128)(2,1)} %param.20), kind=kOutput, calls=%fused_computation.3 | convolution fusion | flops 1879965696 | bytes 16777216 | tf_op jit(solution)/shard_map/dot_general | solution.py:109
  552.6 7.3 %convolution_convert_fusion.1 = bf16[128,7168]{1,0:T(8,128)(2,1)S(1)} fusion(bf16[128,1024]{1,0:T(8,128)(2,1)S(1)} %reshape.82, bf16[1024,7168]{1,0:T(8,128)(2,1)} %param.19), kind=kOutput, calls=%fused_computation.4 | convolution fusion | flops 1879965696 | bytes 16777216 | tf_op jit(solution)/shard_map/dot_general | solution.py:108
  559.9 2.0 pad_maximum_fusion
  562.0 42.4 %reduce-scatter.17.cloned.1.call-done = bf16[16,14336]{1,0:T(8,128)(2,1)} async-done(((bf16[128,14336]{1,0:T(8,128)(2,1)}), bf16[16,14336]{1,0:T(8,128)(2,1)}) %reduce-scatter.17.cloned.1.call-update) | async-done | bytes 458768 | tf_op jit(solution)/shard_map/reduce_scatter | solution.py:105
  604.4 1.1 convert_element_type.107
  605.5 0.8 fusion.18
  606.4 25.3 %all-gather.7.cloned.1.call-done = bf16[128,7168]{1,0:T(8,128)(2,1)} async-done(((bf16[16,7168]{1,0:T(8,128)(2,1)}), bf16[128,7168]{1,0:T(8,128)(2,1)}) %all-gather.7.cloned.1.call-update) | async-done | bytes 1835024 | tf_op jit(solution)/shard_map/all_gather | solution.py:121
  631.7 7.8 %convolution_convert_fusion.6 = bf16[128,1024]{1,0:T(8,128)(2,1)S(1)} fusion(bf16[128,7168]{1,0:T(8,128)(2,1)} %all-gather.7.cloned.1.call-done, bf16[7168,1024]{1,0:T(8,128)(2,1)} %param.21), kind=kOutput, calls=%fused_computation.13 | convolution fusion | flops 1879179264 | bytes 16777216 | tf_op jit(solution)/shard_map/dot_general | solution.py:120
  639.6 0.9 copy.47
  640.5 23.8 %reduce-scatter.23.cloned.1.call-done = bf16[8,1,4,1024]{3,0,2,1:T(8,128)(2,1)} async-done(((bf16[8,4,4,1024]{3,0,2,1:T(8,128)(2,1)}), bf16[8,1,4,1024]{3,0,2,1:T(8,128)(2,1)}) %reduce-scatter.23.cloned.1.call-update) | async-done | bytes 65552
  664.3 0.9 fusion.26
  665.2 10.3 %all_to_all.28 = bf16[8,1,4,1024]{3,2,1,0:T(4,128)(2,1)S(1)} all-to-all(bf16[8,1,4,1024]{3,2,1,0:T(4,128)(2,1)S(1)} %copy.48), channel_id=1, replica_groups=mesh['row'=8,'col'=4] {'row'}, dimensions={0} | all-to-all | bytes 131072 | tf_op jit(solution)/shard_map/all_to_all | solution.py:130
  675.9 0.7 add_convert_fusion
  (48 shorter events, 2.1 us)
Async XLA Ops:
  6.5 317.0 %all-gather.9.cloned.1.call-start = ((), (), s32[]{:S(2)}) async-start(), calls=%async_computation.13 | async-start | bytes 2359296 | tf_op jit(solution)/shard_map/all_gather | solution.py:54
  294.6 39.4 %copy-start.4 = (bf16[1024]{0:T(1024)(128)(2,1)S(1)}, bf16[1024]{0:T(1024)(128)(2,1)}, u32[]{:S(2)}) copy-start(bf16[1024]{0:T(1024)(128)(2,1)} %param.13) | copy-start | bytes 6148
  294.6 63.1 %reduce-scatter.19.cloned.1.call-start = ((), (), s32[]{:S(2)}) async-start(), calls=%async_computation.14 | async-start | bytes 327680
  333.9 85.8 %reduce-scatter.13.cloned.1.call-start = ((), (), s32[]{:S(2)}) async-start(), calls=%async_computation.8 | async-start | bytes 1179648 | tf_op jit(solution)/shard_map/reduce_scatter | solution.py:75
  384.8 3.5 copy-start
  390.1 51.7 %all-gather.5.cloned.1.call-start = ((), (), s32[]{:S(2)}) async-start(), calls=%async_computation.9 | async-start | bytes 1179648 | tf_op jit(solution)/shard_map/all_gather | solution.py:87
  419.7 54.8 %reduce-scatter.15.cloned.1.call-start = ((), (), s32[]{:S(2)}) async-start(), calls=%async_computation.10 | async-start | bytes 589824 | tf_op jit(solution)/shard_map/reduce_scatter | solution.py:68
  423.5 94.4 %reduce-scatter.21.cloned.1.call-start = ((), (), s32[]{:S(2)}) async-start(), calls=%async_computation.15 | async-start | bytes 327680
  475.7 19.8 %copy-start.5 = (bf16[1024]{0:T(1024)(128)(2,1)S(1)}, bf16[1024]{0:T(1024)(128)(2,1)}, u32[]{:S(2)}) copy-start(bf16[1024]{0:T(1024)(128)(2,1)} %param.18) | copy-start | bytes 6148
  475.7 42.2 %copy-start.1 = (bf16[8,1,4,1024]{3,0,2,1:T(8,128)(2,1)S(1)}, bf16[8,1,4,1024]{3,0,2,1:T(8,128)(2,1)}, u32[]{:S(2)}) copy-start(bf16[8,1,4,1024]{3,0,2,1:T(8,128)(2,1)} %reduce-scatter.19.cloned.1.call-done) | copy-start | bytes 196612
  495.4 108.9 %reduce-scatter.17.cloned.1.call-start = ((), (), s32[]{:S(2)}) async-start(), calls=%async_computation.11 | async-start | bytes 4128768 | tf_op jit(solution)/shard_map/reduce_scatter | solution.py:105
  561.9 69.8 %all-gather.7.cloned.1.call-start = ((), (), s32[]{:S(2)}) async-start(), calls=%async_computation.12 | async-start | bytes 2064384 | tf_op jit(solution)/shard_map/all_gather | solution.py:121
  606.3 58.0 %copy-start.3 = (bf16[8,1,4,1024]{3,0,2,1:T(8,128)(2,1)S(1)}, bf16[8,1,4,1024]{3,0,2,1:T(8,128)(2,1)}, u32[]{:S(2)}) copy-start(bf16[8,1,4,1024]{3,0,2,1:T(8,128)(2,1)} %reduce-scatter.21.cloned.1.call-done) | copy-start | bytes 196612
  606.3 69.5 %copy-start.2 = (bf16[16,8192]{1,0:T(8,128)(2,1)S(1)}, bf16[16,8192]{1,0:T(8,128)(2,1)}, u32[]{:S(2)}) copy-start(bf16[16,8192]{1,0:T(8,128)(2,1)} %param.11) | copy-start | bytes 786436
  606.3 58.0 %reduce-scatter.23.cloned.1.call-start = ((), (), s32[]{:S(2)}) async-start(), calls=%async_computation.16 | async-start | bytes 327680
Sparse Core Ops, SparseCore 0:
  294.7 28.8 all-gather.8
  334.0 23.5 reduce-scatter.18
  390.2 29.4 reduce-scatter.12
  421.2 20.4 all-gather.4
  443.9 30.5 reduce-scatter.14
  495.6 22.3 reduce-scatter.20
  562.0 42.2 reduce-scatter.16
  606.4 25.2 all-gather.6
  640.6 23.6 reduce-scatter.22
where the time goes:
time: 685 us; the launch traced here: 683 us
  waiting for transfers between devices  246 us (36%)
  other arithmetic  190 us (28%)
  local copies, waits for them, and re-layouts  103 us (15%)
  blocking collectives  86.2 us (13%)
  matrix products  44.8 us (7%)
  between operations  13.5 us (2%)
    unnamed x1, other arithmetic  179 us
    unnamed x12, waiting for transfers between devices  70 us
    reduce_scatter x1, waiting for transfers between devices, on_device(): lax.psum_scatter(jnp.concatenate([jnp.dot(slab, w_gate, preferred_element...  42.4 us
    unnamed x16, local copies, waits for them, and re-layouts  41.3 us
    all_to_all x3, local copies, waits for them, and re-layouts, on_device(): lax.all_to_all(grouped, 'col', split_axis=3, concat_axis=1, tiled=True)  31.7 us
    reduce_scatter x1, waiting for transfers between devices, on_device(): lax.psum_scatter(jnp.dot(slab, w_query, preferred_element_type=jnp.float3...  31.5 us
    reduce_scatter x1, waiting for transfers between devices, on_device(): lax.psum_scatter(jnp.concatenate([jnp.dot(slab, w_key, preferred_element_...  29.6 us
    all_gather x1, waiting for transfers between devices, on_device(): piece = lax.all_gather(spread, 'row', axis=0, tiled=True)  28.9 us
  transfers between devices with their start and end apart: 9, of which 9 were waited for; matrix products, arithmetic and copies ran while one was open for 1% of the time, Pallas kernels for 0%

commit v1 on v0

--- a/solution.py
+++ b/solution.py
@@ -1,6 +1,10 @@
+import functools
+
 import jax
 import jax.numpy as jnp
 from jax import lax
+from jax.experimental import pallas as pl
+from jax.experimental.pallas import tpu as pltpu
 from jax.sharding import PartitionSpec as P
 
 D = 8192
@@ -41,7 +45,7 @@
     return mixed.astype(jnp.bfloat16).reshape(query_count, -1)
 
 
-def on_device(
+def by_collectives(
     chars, pool_weight, gain_attn, w_query, w_key, w_value, w_out, gain_ffn, w_gate, w_up, w_down
 ):
     rows_count = lax.axis_size("row")
@@ -132,6 +136,484 @@
     return (chars.astype(jnp.float32) + expanded.astype(jnp.float32)).astype(jnp.bfloat16)
 
 
+MESH = pl.DeviceIdType.MESH
+BF = jnp.bfloat16
+F32 = jnp.float32
+SLOTS = 20
+SUB = 16
+
+
+def one_hot(shape, test):
+    rows_at = lax.broadcasted_iota(jnp.int32, shape, 0)
+    cols_at = lax.broadcasted_iota(jnp.int32, shape, 1)
+    return jnp.where(test(rows_at, cols_at), 1.0, 0.0).astype(BF)
+
+
+def mm(left, right):
+    return jnp.dot(left, right, preferred_element_type=F32)
+
+
+def layer_kernel(
+    sizes, chars, pool_w, gain_a, wq, wk, wv, wo, gain_f, wg, wu, wd, out,
+    ring, ring_sem,
+    stage, xin, xall, part, crecv, hall, scaled, resid,
+    sq, sqrecv, factor,
+    qp, qsib, qsum, qz, mixall,
+    gp, gsib, gsum, gz, act, dacc,
+    fsend, frecv,
+    a2a_s, a2a_r, xz_s, xz_r, xs_s, xs_r, rs_s, rs_r, ag_s, ag_r, sq_s, sq_r,
+    qs_s, qs_r, qz_s, qz_r, mz_s, mz_r, ms_s, ms_r,
+    gs_s, gs_r, gz_s, gz_r, az_s, az_r, as_s, as_r, fin_s, fin_r,
+):
+    rows, cols, tokens, width, here, chunks = sizes
+    deep = rows // 2
+    quarter = SUB // here
+    piece = chars.shape[1] // quarter
+    share = tokens // cols
+    mine = tokens // rows
+    half = tokens // 2
+    head_cols = wq.shape[1] // rows
+    tile = head_cols
+    row = lax.axis_index("row")
+    col = lax.axis_index("col")
+    level = lax.div(row, 2)
+    core = lax.rem(row, 2)
+    other = 1 - core
+    sibling = (level * 2 + other, col)
+    pending = []
+
+    def send(source, target, s_sem, r_sem, where):
+        copy = pltpu.make_async_remote_copy(
+            src_ref=source, dst_ref=target, send_sem=s_sem, recv_sem=r_sem,
+            device_id=where, device_id_type=MESH,
+        )
+        copy.start()
+        pending.append(copy)
+        return copy
+
+    def col_at(d):
+        return lax.rem(col + d, cols)
+
+    def level_at(d):
+        return lax.rem(level + d, deep)
+
+    def row_at(d):
+        return lax.rem(row + d, rows)
+
+    blocks = [(pool_w, i, 0) for i in range(pool_w.shape[0] // width)]
+    n_pool = len(blocks)
+    for weight in (wq, wk, wv):
+        blocks += [(weight, 0, i) for i in range(weight.shape[1] // width)]
+    n_qkv = len(blocks)
+    blocks += [(wo, i, 0) for i in range(wo.shape[0] // width)]
+    n_out = len(blocks)
+    for i in range(chunks):
+        blocks += [(wg, 0, i), (wu, 0, i)]
+    n_up = len(blocks)
+    blocks += [(wd, i, 0) for i in range(chunks)]
+
+    def fetch(i):
+        ref, down, across = blocks[i]
+        return pltpu.make_async_copy(
+            ref.at[pl.ds(down * width, width), pl.ds(across * width, width)],
+            ring.at[i % SLOTS], ring_sem.at[i],
+        )
+
+    def fetch_after(first, last):
+        for i in range(first, last):
+            if i + SLOTS < len(blocks):
+                fetch(i + SLOTS).start()
+
+    for i in range(min(SLOTS, len(blocks))):
+        fetch(i).start()
+
+    barrier = pltpu.get_barrier_semaphore()
+    for d in range(1, cols):
+        pl.semaphore_signal(barrier, inc=1, device_id=(row, col_at(d)), device_id_type=MESH)
+    for d in range(1, rows):
+        pl.semaphore_signal(barrier, inc=1, device_id=(row_at(d), col), device_id_type=MESH)
+
+    for q in range(quarter):
+        pick = one_hot(
+            (cols * SUB, here * cols),
+            lambda i, m: (m == (i % here) * cols + i // SUB) & ((i % SUB) // here == q),
+        )
+        term = mm(pick, chars[:, q * piece:(q + 1) * piece])
+        if q == 0:
+            total = term
+        else:
+            total = total + term
+    stage[...] = total.astype(BF)
+    at = pl.multiple_of(col * SUB, SUB)
+    xin[pl.ds(at, SUB), :] = stage[pl.ds(at, SUB), :]
+    pl.semaphore_wait(barrier, cols + rows - 2)
+    copies = []
+    for d in range(1, cols):
+        copies.append(send(
+            stage.at[pl.ds(pl.multiple_of(col_at(d) * SUB, SUB), SUB), :], xin.at[pl.ds(at, SUB), :],
+            a2a_s.at[d], a2a_r.at[d], (row, col_at(d)),
+        ))
+    for copy in copies:
+        copy.wait_recv()
+    here_at = pl.multiple_of(row * mine, mine)
+    for q in range(quarter):
+        pick = one_hot(
+            (mine, cols * SUB),
+            lambda i, m: (m // SUB == i // here) & (m % here == i % here) & ((m % SUB) // here == q),
+        )
+        xall[pl.ds(here_at, mine), q * piece:(q + 1) * piece] = mm(pick, xin[...]).astype(BF)
+
+    def x_rows(level_of, core_of):
+        return xall.at[pl.ds(pl.multiple_of((level_of * 2 + core_of) * mine, mine), mine), :]
+
+    copies = []
+    for d in range(1, deep):
+        copies.append(send(
+            x_rows(level, core), x_rows(level, core), xz_s.at[d], xz_r.at[d], (level_at(d) * 2 + core, col),
+        ))
+    sibs = [send(x_rows(level, core), x_rows(level, core), xs_s.at[0], xs_r.at[0], sibling)]
+    for d in range(1, deep):
+        copies[d - 1].wait_recv()
+        source = level_at(deep - d)
+        sibs.append(send(x_rows(source, core), x_rows(source, core), xs_s.at[d], xs_r.at[d], sibling))
+    for copy in sibs:
+        copy.wait_recv()
+
+    for i in range(n_pool):
+        fetch(i).wait()
+    order = one_hot(
+        (tokens, tokens),
+        lambda i, m: m == ((i % share) // here) * mine + (i // share) * here + i % here,
+    )
+
+    @pl.loop(0, width // tile)
+    def _(n):
+        across = pl.ds(pl.multiple_of(n * tile, tile), tile)
+        total = jnp.zeros((tokens, tile), F32)
+        for i in range(n_pool):
+            total = total + mm(xall[:, i * width:(i + 1) * width], ring[i % SLOTS, :, across])
+        part[0, :, across] = mm(order, total.astype(BF)).astype(BF)
+
+    fetch_after(0, n_pool)
+    share_at = pl.multiple_of(col * share, share)
+    my_share = pl.ds(share_at, share)
+
+    def reduce_cols(step):
+        copies = []
+        for d in range(1, cols):
+            copies.append(send(
+                part.at[step, pl.ds(pl.multiple_of(col_at(d) * share, share), share), :],
+                crecv.at[step, d - 1], rs_s.at[step, d], rs_r.at[step, d], (row, col_at(d)),
+            ))
+        for copy in copies:
+            copy.wait_recv()
+        total = part[step, my_share, :].astype(F32)
+        for d in range(1, cols):
+            total = total + crecv[step, d - 1].astype(F32)
+        return total
+
+    def spread_norm(step, values, gain):
+        resid[...] = values
+        hall[step, my_share, :] = values
+        copies = []
+        for d in range(1, cols):
+            copies.append(send(
+                hall.at[step, my_share, :], hall.at[step, my_share, :],
+                ag_s.at[step, d], ag_r.at[step, d], (row, col_at(d)),
+            ))
+        for copy in copies:
+            copy.wait_recv()
+        whole = hall[step].astype(F32)
+        scaled[...] = (whole * gain[...].astype(F32)).astype(BF)
+        squares = jnp.sum(whole * whole, axis=1, keepdims=True)
+        flat = jnp.broadcast_to(squares, (tokens, tokens)).T
+        sq[step] = flat[:8]
+        return [
+            send(sq.at[step], sqrecv.at[step, d - 1], sq_s.at[step, d], sq_r.at[step, d], (row_at(d), col))
+            for d in range(1, rows)
+        ]
+
+    def take_factor(step, copies):
+        for copy in copies:
+            copy.wait_recv()
+        total = sq[step]
+        for d in range(1, rows):
+            total = total + sqrecv[step, d - 1]
+        line = lax.rsqrt(total / (rows * width) + EPS)
+        factor[...] = jnp.broadcast_to(line[:1], (tokens, tokens)).T
+
+    sq_copies = spread_norm(0, reduce_cols(0).astype(BF), gain_a)
+
+    per = width // tile
+    for kind in range(3):
+        for b in range(wq.shape[1] // width):
+            i = n_pool + kind * (wq.shape[1] // width) + b
+            fetch(i).wait()
+
+            @pl.loop(0, per)
+            def _(n):
+                owner = b * per + n
+                across = pl.ds(pl.multiple_of(n * tile, tile), tile)
+                qp[lax.rem(owner, 2), lax.div(owner, 2), :, kind * tile:(kind + 1) * tile] = mm(
+                    scaled[...], ring[i % SLOTS, :, across]
+                ).astype(BF)
+
+    fetch_after(n_pool, n_qkv)
+    send(qp.at[other], qsib, qs_s, qs_r, sibling).wait_recv()
+    copies = []
+    for d in list(range(1, deep)) + [0]:
+        there = level_at(d)
+        qsum[there] = (qp[core, there].astype(F32) + qsib[there].astype(F32)).astype(BF)
+        if d:
+            copies.append(send(
+                qsum.at[there], qz.at[d - 1], qz_s.at[d], qz_r.at[d], (there * 2 + core, col)
+            ))
+    take_factor(0, sq_copies)
+    for copy in copies:
+        copy.wait_recv()
+    places_i = lax.broadcasted_iota(jnp.int32, (tokens, tokens), 0)
+    places_j = lax.broadcasted_iota(jnp.int32, (tokens, tokens), 1)
+
+    def true_place(i):
+        return ((i % share) // here) * mine + (i // share) * here + i % here
+
+    allowed = true_place(places_i) >= true_place(places_j)
+
+    def head_part(at):
+        total = qsum[level, :, at:at + HD].astype(F32)
+        for d in range(1, deep):
+            total = total + qz[d - 1, :, at:at + HD].astype(F32)
+        return (total * factor[:, :1]).astype(BF)
+
+    for h in range(tile // HD):
+        queries = head_part(h * HD)
+        keys = head_part(tile + h * HD)
+        values = head_part(2 * tile + h * HD)
+        scores = lax.dot_general(
+            queries, keys, (((1,), (1,)), ((), ())), preferred_element_type=F32
+        ) * HD ** (-0.5)
+        scores = jnp.where(allowed, scores, -1e30)
+        weights = jnp.exp(scores - jnp.max(scores, axis=1, keepdims=True))
+        weights = (weights / jnp.sum(weights, axis=1, keepdims=True)).astype(BF)
+        mixall[row, :, h * HD:(h + 1) * HD] = mm(weights, values).astype(BF)
+    copies = [
+        send(mixall.at[row], mixall.at[row], mz_s.at[d], mz_r.at[d], (level_at(d) * 2 + core, col))
+        for d in range(1, deep)
+    ]
+    sibs = [send(mixall.at[row], mixall.at[row], ms_s.at[0], ms_r.at[0], sibling)]
+    for d in range(1, deep):
+        copies[d - 1].wait_recv()
+        source = level_at(deep - d) * 2 + core
+        sibs.append(send(mixall.at[source], mixall.at[source], ms_s.at[d], ms_r.at[d], sibling))
+    for copy in sibs:
+        copy.wait_recv()
+
+    for i in range(n_qkv, n_out):
+        fetch(i).wait()
+
+    @pl.loop(0, width // tile)
+    def _(n):
+        across = pl.ds(pl.multiple_of(n * tile, tile), tile)
+        total = jnp.zeros((tokens, tile), F32)
+        for r in range(rows):
+            i = n_qkv + r * tile // width
+            down = r * tile % width
+            total = total + mm(mixall[r], ring[i % SLOTS, down:down + tile, across])
+        part[1, :, across] = total.astype(BF)
+
+    fetch_after(n_qkv, n_out)
+    total = reduce_cols(1)
+    sq_copies = spread_norm(1, (resid[...].astype(F32) + total).astype(BF), gain_f)
+
+    def rows_of(level_of):
+        return pl.ds(pl.multiple_of(level_of * mine, mine), mine)
+
+    def half_of(core_of):
+        return pl.ds(pl.multiple_of(core_of * half, half), half)
+
+    def product(c):
+        for k in range(2):
+            i = n_out + 2 * c + k
+            fetch(i).wait()
+
+            @pl.loop(0, width // tile)
+            def _(n):
+                across = pl.ds(pl.multiple_of(n * tile, tile), tile)
+                to = pl.ds(pl.multiple_of(k * width + n * tile, tile), tile)
+                gp[c, :, to] = mm(scaled[...], ring[i % SLOTS, :, across]).astype(BF)
+
+        fetch_after(n_out + 2 * c, n_out + 2 * c + 2)
+        return send(gp.at[c, half_of(other), :], gsib.at[c], gs_s.at[c], gs_r.at[c], sibling)
+
+    def presum(c, copy):
+        copy.wait_recv()
+        gsum[c] = (gp[c, half_of(core), :].astype(F32) + gsib[c].astype(F32)).astype(BF)
+        return [
+            send(
+                gsum.at[c, rows_of(level_at(d)), :], gz.at[c, d - 1],
+                gz_s.at[c, d], gz_r.at[c, d], (level_at(d) * 2 + core, col),
+            )
+            for d in range(1, deep)
+        ]
+
+    own_at = pl.multiple_of(core * half + level * mine, mine)
+
+    def activate(c, copies):
+        for copy in copies:
+            copy.wait_recv()
+        total = gsum[c, rows_of(level), :].astype(F32)
+        for d in range(1, deep):
+            total = total + gz[c, d - 1].astype(F32)
+        total = total * factor[pl.ds(own_at, mine), :1]
+        gate, up = total[:, :width], total[:, width:]
+        act[c, pl.ds(own_at, mine), :] = (gate * (1.0 / (1.0 + jnp.exp(-gate))) * up).astype(BF)
+        return [
+            send(
+                act.at[c, pl.ds(own_at, mine), :], act.at[c, pl.ds(own_at, mine), :],
+                az_s.at[c, d], az_r.at[c, d], (level_at(d) * 2 + core, col),
+            )
+            for d in range(1, deep)
+        ]
+
+    def forward(c, copies):
+        for copy in copies:
+            copy.wait_recv()
+        return send(act.at[c, half_of(core), :], act.at[c, half_of(core), :], as_s.at[c], as_r.at[c], sibling)
+
+    def down(c, copy):
+        copy.wait_recv()
+        i = n_up + c
+        fetch(i).wait()
+
+        @pl.loop(0, width // tile)
+        def _(n):
+            across = pl.ds(pl.multiple_of(n * tile, tile), tile)
+            term = mm(act[c], ring[i % SLOTS, :, across])
+            if c:
+                term = term + dacc[:, across]
+            if c < chunks - 1:
+                dacc[:, across] = term
+            else:
+                part[2, :, across] = term.astype(BF)
+
+    first, second, third, fourth = {}, {}, {}, {}
+    for c in range(chunks + 1):
+        if c < chunks:
+            first[c] = product(c)
+        if c:
+            second[c - 1] = presum(c - 1, first[c - 1])
+    take_factor(1, sq_copies)
+    for c in range(chunks + 2):
+        if c < chunks:
+            third[c] = activate(c, second[c])
+        if 1 <= c <= chunks:
+            fourth[c - 1] = forward(c - 1, third[c - 1])
+        if c >= 2:
+            down(c - 2, fourth[c - 2])
+
+    total = reduce_cols(2)
+    final = (resid[...].astype(F32) + total).astype(BF)
+
+    strip = width // quarter
+    for q in range(quarter):
+        pick = one_hot(
+            (rows * SUB, share),
+            lambda i, m: (i // SUB == m // here) & (i % here == m % here) & ((i % SUB) // here == q),
+        )
+        term = mm(pick, final[:, q * strip:(q + 1) * strip])
+        if q == 0:
+            total = term
+        else:
+            total = total + term
+    fsend[...] = total.astype(BF)
+    me_at = pl.multiple_of(row * SUB, SUB)
+    frecv[pl.ds(me_at, SUB), :] = fsend[pl.ds(me_at, SUB), :]
+    copies = []
+    for d in range(1, rows):
+        copies.append(send(
+            fsend.at[pl.ds(pl.multiple_of(row_at(d) * SUB, SUB), SUB), :], frecv.at[pl.ds(me_at, SUB), :],
+            fin_s.at[d], fin_r.at[d], (row_at(d), col),
+        ))
+    for copy in copies:
+        copy.wait_recv()
+    for q in range(quarter):
+        pick = one_hot(
+            (here * cols, SUB), lambda i, m: (m % here == i // cols) & (m // here == q)
+        )
+        for s in range(rows):
+            to = slice(s * width + q * strip, s * width + (q + 1) * strip)
+            out[:, to] = (chars[:, to].astype(F32) + mm(pick, frecv[s * SUB:(s + 1) * SUB, :])).astype(BF)
+    for copy in pending:
+        copy.wait_send()
+
+
+def fused_layer(chars, pool_w, gain_a, wq, wk, wv, wo, gain_f, wg, wu, wd):
+    rows = lax.axis_size("row")
+    cols = lax.axis_size("col")
+    width = pool_w.shape[1]
+    here = chars.shape[0] // POOL
+    tokens = here * rows * cols
+    chunks = wg.shape[1] // width
+    deep = rows // 2
+    share, mine, half = tokens // cols, tokens // rows, tokens // 2
+    tile = wq.shape[1] // rows
+    piece = chars.shape[1] * here // SUB
+    dma = pltpu.SemaphoreType.DMA
+    scratch = [
+        pltpu.VMEM((SLOTS, width, width), BF), dma((64,)),
+        pltpu.VMEM((cols * SUB, piece), BF), pltpu.VMEM((cols * SUB, piece), BF),
+        pltpu.VMEM((tokens, chars.shape[1]), BF),
+        pltpu.VMEM((3, tokens, width), BF), pltpu.VMEM((3, cols - 1, share, width), BF),
+        pltpu.VMEM((2, tokens, width), BF), pltpu.VMEM((tokens, width), BF), pltpu.VMEM((share, width), BF),
+        pltpu.VMEM((2, 8, tokens), F32), pltpu.VMEM((2, rows - 1, 8, tokens), F32), pltpu.VMEM((tokens, tokens), F32),
+        pltpu.VMEM((2, deep, tokens, 3 * tile), BF), pltpu.VMEM((deep, tokens, 3 * tile), BF),
+        pltpu.VMEM((deep, tokens, 3 * tile), BF), pltpu.VMEM((deep - 1, tokens, 3 * tile), BF),
+        pltpu.VMEM((rows, tokens, tile), BF),
+        pltpu.VMEM((chunks, tokens, 2 * width), BF), pltpu.VMEM((chunks, half, 2 * width), BF),
+        pltpu.VMEM((chunks, half, 2 * width), BF), pltpu.VMEM((chunks, deep - 1, mine, 2 * width), BF),
+        pltpu.VMEM((chunks, tokens, width), BF), pltpu.VMEM((tokens, width), F32),
+        pltpu.VMEM((rows * SUB, width * here // SUB), BF), pltpu.VMEM((rows * SUB, width * here // SUB), BF),
+        dma((cols,)), dma((cols,)), dma((deep,)), dma((deep,)), dma((deep,)), dma((deep,)),
+        dma((3, cols)), dma((3, cols)), dma((2, cols)), dma((2, cols)), dma((2, rows)), dma((2, rows)),
+        dma, dma, dma((deep,)), dma((deep,)), dma((deep,)), dma((deep,)), dma((deep,)), dma((deep,)),
+        dma((chunks,)), dma((chunks,)), dma((chunks, deep)), dma((chunks, deep)),
+        dma((chunks, deep)), dma((chunks, deep)), dma((chunks,)), dma((chunks,)), dma((rows,)), dma((rows,)),
+    ]
+    vmem, hbm = pl.BlockSpec(memory_space=pltpu.VMEM), pl.BlockSpec(memory_space=pl.ANY)
+    return pl.pallas_call(
+        functools.partial(layer_kernel, (rows, cols, tokens, width, here, chunks)),
+        out_shape=jax.ShapeDtypeStruct(chars.shape, chars.dtype),
+        in_specs=[vmem, hbm, vmem, hbm, hbm, hbm, hbm, vmem, hbm, hbm, hbm],
+        out_specs=vmem,
+        scratch_shapes=scratch,
+        compiler_params=pltpu.CompilerParams(
+            collective_id=0, has_side_effects=True, vmem_limit_bytes=63 * 1024 * 1024
+        ),
+    )(chars, pool_w, gain_a.reshape(1, -1), wq, wk, wv, wo, gain_f.reshape(1, -1), wg, wu, wd)
+
+
+def fits(chars, pool_w, wq, wg):
+    rows, cols = lax.axis_size("row"), lax.axis_size("col")
+    width = pool_w.shape[1]
+    here = chars.shape[0] // POOL
+    tokens = here * rows * cols
+    return (
+        cols == POOL and rows % 2 == 0 and tokens == HD and SUB % here == 0
+        and (wq.shape[1] // HD) % rows == 0 and tokens // rows == SUB
+        and wq.shape[1] % width == 0 and wg.shape[1] % width == 0
+        and width % (wq.shape[1] // rows) == 0
+    )
+
+
+def on_device(
+    chars, pool_weight, gain_attn, w_query, w_key, w_value, w_out, gain_ffn, w_gate, w_up, w_down
+):
+    args = (chars, pool_weight, gain_attn, w_query, w_key, w_value, w_out, gain_ffn, w_gate, w_up, w_down)
+    if fits(chars, pool_weight, w_query, w_gate):
+        return fused_layer(*args)
+    return by_collectives(*args)
+
+
 def solution(mesh):
     return jax.shard_map(
         on_device,

time: 685 us -> 187 us (0.27)
  waiting for transfers between devices: 246 us -> 0 us
  other arithmetic: 190 us -> 0 us
  Pallas kernels: 0 us -> 182 us
  local copies, waits for them, and re-layouts: 103 us -> 4.22 us
  blocking collectives: 86.2 us -> 0 us
  matrix products: 44.8 us -> 0 us
  between operations: 13.5 us -> 0.01 us
    pallas_call x0 -> x1, Pallas kernels: none -> 182 us  [fused_layer(): pl.pallas_call(functools.partial(layer_kernel, (rows, cols, tokens, width...]
    unnamed x1 -> x0, other arithmetic: 179 us -> none
    reduce_scatter x3 -> x0, waiting for transfers between devices: 103 us -> none  [the longest x1 42.4 us: on_device(): lax.psum_scatter(jnp.concatenate([jnp.dot(slab, w_gate, preferred_element...]
    all_gather x3 -> x0, waiting for transfers between devices: 72.4 us -> none  [the longest x1 28.9 us: on_device(): piece = lax.all_gather(spread, 'row', axis=0, tiled=True)]
    unnamed x12 -> x0, waiting for transfers between devices: 70 us -> none
    dot_general x10 -> x0, matrix products: 44.8 us -> none  [the longest x1 10.4 us: on_device(): jnp.dot(piece.reshape(-1, piece.shape[3]), pool_weight, preferred_element...]
    unnamed x16 -> x1, local copies, waits for them, and re-layouts: 41.3 us -> 1.67 us
    all_gather x3 -> x0, blocking collectives: 33.5 us -> none  [the longest x1 15 us: on_device(): lax.all_gather(mixed, 'row', axis=0, tiled=True)]
  transfers between devices with their start and end apart: 9 -> 0, of which waited for: 9 -> 0; matrix products, arithmetic and copies ran while one was open for 1% -> 0% of each run, Pallas kernels for 0% -> 0%
where the time goes in v1:
time: 187 us
  Pallas kernels  182 us (97%)
  local copies, waits for them, and re-layouts  4.22 us (2%)
    pallas_call x1, Pallas kernels, fused_layer(): pl.pallas_call(functools.partial(layer_kernel, (rows, cols, tokens, width...  182 us

profile of v1, /device:TPU:0, one launch (start us, length us, event | category | flops | bytes accessed | tf_op | source)
XLA Modules:
  0.0 186.6 jit_solution(6732482609232538873)
XLA Ops:
  0.0 1.3 reshape.6.gain_a
  1.3 1.3 reshape.7.gain_f
  2.6 182.3 %shard_map.109 = bf16[16,8192]{1,0:T(8,128)(2,1)} custom-call(bf16[16,8192]{1,0:T(8,128)(2,1)} %chars.1, bf16[8192,1024]{1,0:T(8,128)(2,1)} %pool_w.1, bf16[1,1024]{1,0:T(2,128)(2,1)} %reshape.6.gain_a, bf16[1024,2048]{1,0:T(8,128)(2,1)} %wq.1, bf16[1024,2048]{1,0:T(8,128)(2,1)} %wk.1, bf16[1024,2048]{1,0:T(8,128)(2,1)} %wv.1, bf16[2048,1024]{1,0:T(8,128)(2,1)} %wo.1, ...), custom_call_target="tpu_custom_call" | custom-call | tf_op jit(solution)/shard_map/pallas_call | solution.py:583
  184.9 1.7 copy.13

commit v2 on v1

--- a/solution.py
+++ b/solution.py
@@ -256,44 +256,61 @@
     for copy in copies:
         copy.wait_recv()
     here_at = pl.multiple_of(row * mine, mine)
+
+    def x_rows(level_of, core_of, q):
+        at = pl.multiple_of((level_of * 2 + core_of) * mine, mine)
+        return xall.at[pl.ds(at, mine), q * piece:(q + 1) * piece]
+
+    across_z, sibs = {}, {}
     for q in range(quarter):
         pick = one_hot(
             (mine, cols * SUB),
             lambda i, m: (m // SUB == i // here) & (m % here == i % here) & ((m % SUB) // here == q),
         )
         xall[pl.ds(here_at, mine), q * piece:(q + 1) * piece] = mm(pick, xin[...]).astype(BF)
-
-    def x_rows(level_of, core_of):
-        return xall.at[pl.ds(pl.multiple_of((level_of * 2 + core_of) * mine, mine), mine), :]
-
-    copies = []
-    for d in range(1, deep):
-        copies.append(send(
-            x_rows(level, core), x_rows(level, core), xz_s.at[d], xz_r.at[d], (level_at(d) * 2 + core, col),
-        ))
-    sibs = [send(x_rows(level, core), x_rows(level, core), xs_s.at[0], xs_r.at[0], sibling)]
-    for d in range(1, deep):
-        copies[d - 1].wait_recv()
-        source = level_at(deep - d)
-        sibs.append(send(x_rows(source, core), x_rows(source, core), xs_s.at[d], xs_r.at[d], sibling))
-    for copy in sibs:
-        copy.wait_recv()
-
-    for i in range(n_pool):
-        fetch(i).wait()
+        mine_q = x_rows(level, core, q)
+        for d in range(1, deep):
+            across_z[q, d] = send(
+                mine_q, mine_q, xz_s.at[q, d], xz_r.at[q, d], (level_at(d) * 2 + core, col)
+            )
+        sibs[q] = [send(mine_q, mine_q, xs_s.at[q, 0], xs_r.at[q, 0], sibling)]
+
+    def forward_piece(q):
+        for d in range(1, deep):
+            across_z[q, d].wait_recv()
+            came = x_rows(level_at(deep - d), core, q)
+            sibs[q].append(send(came, came, xs_s.at[q, d], xs_r.at[q, d], sibling))
+
+    def pool_piece(q):
+        for copy in sibs[q]:
+            copy.wait_recv()
+        ids = range(q * n_pool // quarter, (q + 1) * n_pool // quarter)
+        for i in ids:
+            fetch(i).wait()
+
+        @pl.loop(0, width // tile)
+        def _(n):
+            across = pl.ds(pl.multiple_of(n * tile, tile), tile)
+            if q:
+                total = dacc[:, across]
+            else:
+                total = jnp.zeros((tokens, tile), F32)
+            for i in ids:
+                total = total + mm(xall[:, i * width:(i + 1) * width], ring[i % SLOTS, :, across])
+            if q < quarter - 1:
+                dacc[:, across] = total
+            else:
+                part[0, :, across] = mm(order, total.astype(BF)).astype(BF)
+
     order = one_hot(
         (tokens, tokens),
         lambda i, m: m == ((i % share) // here) * mine + (i // share) * here + i % here,
     )
-
-    @pl.loop(0, width // tile)
-    def _(n):
-        across = pl.ds(pl.multiple_of(n * tile, tile), tile)
-        total = jnp.zeros((tokens, tile), F32)
-        for i in range(n_pool):
-            total = total + mm(xall[:, i * width:(i + 1) * width], ring[i % SLOTS, :, across])
-        part[0, :, across] = mm(order, total.astype(BF)).astype(BF)
-
+    for q in range(quarter + 1):
+        if q < quarter:
+            forward_piece(q)
+        if q:
+            pool_piece(q - 1)
     fetch_after(0, n_pool)
     share_at = pl.multiple_of(col * share, share)
     my_share = pl.ds(share_at, share)
@@ -345,29 +362,41 @@
     sq_copies = spread_norm(0, reduce_cols(0).astype(BF), gain_a)
 
     per = width // tile
-    for kind in range(3):
-        for b in range(wq.shape[1] // width):
-            i = n_pool + kind * (wq.shape[1] // width) + b
+    per_kind = wq.shape[1] // width
+    copies, swaps = [], {}
+
+    def qkv_product(kind):
+        for b in range(per_kind):
+            i = n_pool + kind * per_kind + b
             fetch(i).wait()
 
             @pl.loop(0, per)
             def _(n):
                 owner = b * per + n
                 across = pl.ds(pl.multiple_of(n * tile, tile), tile)
-                qp[lax.rem(owner, 2), lax.div(owner, 2), :, kind * tile:(kind + 1) * tile] = mm(
+                qp[kind, lax.rem(owner, 2), lax.div(owner, 2)] = mm(
                     scaled[...], ring[i % SLOTS, :, across]
                 ).astype(BF)
 
-    fetch_after(n_pool, n_qkv)
-    send(qp.at[other], qsib, qs_s, qs_r, sibling).wait_recv()
-    copies = []
-    for d in list(range(1, deep)) + [0]:
-        there = level_at(d)
-        qsum[there] = (qp[core, there].astype(F32) + qsib[there].astype(F32)).astype(BF)
-        if d:
-            copies.append(send(
-                qsum.at[there], qz.at[d - 1], qz_s.at[d], qz_r.at[d], (there * 2 + core, col)
-            ))
+        fetch_after(n_pool + kind * per_kind, n_pool + (kind + 1) * per_kind)
+        swaps[kind] = send(qp.at[kind, other], qsib.at[kind], qs_s.at[kind], qs_r.at[kind], sibling)
+
+    def qkv_presum(kind):
+        swaps[kind].wait_recv()
+        for d in list(range(1, deep)) + [0]:
+            there = level_at(d)
+            qsum[kind, there] = (qp[kind, core, there].astype(F32) + qsib[kind, there].astype(F32)).astype(BF)
+            if d:
+                copies.append(send(
+                    qsum.at[kind, there], qz.at[kind, d - 1],
+                    qz_s.at[kind, d], qz_r.at[kind, d], (there * 2 + core, col),
+                ))
+
+    for kind in range(4):
+        if kind < 3:
+            qkv_product(kind)
+        if kind:
+            qkv_presum(kind - 1)
     take_factor(0, sq_copies)
     for copy in copies:
         copy.wait_recv()
@@ -379,16 +408,16 @@
 
     allowed = true_place(places_i) >= true_place(places_j)
 
-    def head_part(at):
-        total = qsum[level, :, at:at + HD].astype(F32)
+    def head_part(kind, at):
+        total = qsum[kind, level, :, at:at + HD].astype(F32)
         for d in range(1, deep):
-            total = total + qz[d - 1, :, at:at + HD].astype(F32)
+            total = total + qz[kind, d - 1, :, at:at + HD].astype(F32)
         return (total * factor[:, :1]).astype(BF)
 
     for h in range(tile // HD):
-        queries = head_part(h * HD)
-        keys = head_part(tile + h * HD)
-        values = head_part(2 * tile + h * HD)
+        queries = head_part(0, h * HD)
+        keys = head_part(1, h * HD)
+        values = head_part(2, h * HD)
         scores = lax.dot_general(
             queries, keys, (((1,), (1,)), ((), ())), preferred_element_type=F32
         ) * HD ** (-0.5)
@@ -566,16 +595,16 @@
         pltpu.VMEM((3, tokens, width), BF), pltpu.VMEM((3, cols - 1, share, width), BF),
         pltpu.VMEM((2, tokens, width), BF), pltpu.VMEM((tokens, width), BF), pltpu.VMEM((share, width), BF),
         pltpu.VMEM((2, 8, tokens), F32), pltpu.VMEM((2, rows - 1, 8, tokens), F32), pltpu.VMEM((tokens, tokens), F32),
-        pltpu.VMEM((2, deep, tokens, 3 * tile), BF), pltpu.VMEM((deep, tokens, 3 * tile), BF),
-        pltpu.VMEM((deep, tokens, 3 * tile), BF), pltpu.VMEM((deep - 1, tokens, 3 * tile), BF),
+        pltpu.VMEM((3, 2, deep, tokens, tile), BF), pltpu.VMEM((3, deep, tokens, tile), BF),
+        pltpu.VMEM((3, deep, tokens, tile), BF), pltpu.VMEM((3, deep - 1, tokens, tile), BF),
         pltpu.VMEM((rows, tokens, tile), BF),
         pltpu.VMEM((chunks, tokens, 2 * width), BF), pltpu.VMEM((chunks, half, 2 * width), BF),
         pltpu.VMEM((chunks, half, 2 * width), BF), pltpu.VMEM((chunks, deep - 1, mine, 2 * width), BF),
         pltpu.VMEM((chunks, tokens, width), BF), pltpu.VMEM((tokens, width), F32),
         pltpu.VMEM((rows * SUB, width * here // SUB), BF), pltpu.VMEM((rows * SUB, width * here // SUB), BF),
-        dma((cols,)), dma((cols,)), dma((deep,)), dma((deep,)), dma((deep,)), dma((deep,)),
+        dma((cols,)), dma((cols,)), dma((SUB // here, deep)), dma((SUB // here, deep)), dma((SUB // here, deep)), dma((SUB // here, deep)),
         dma((3, cols)), dma((3, cols)), dma((2, cols)), dma((2, cols)), dma((2, rows)), dma((2, rows)),
-        dma, dma, dma((deep,)), dma((deep,)), dma((deep,)), dma((deep,)), dma((deep,)), dma((deep,)),
+        dma((3,)), dma((3,)), dma((3, deep)), dma((3, deep)), dma((deep,)), dma((deep,)), dma((deep,)), dma((deep,)),
         dma((chunks,)), dma((chunks,)), dma((chunks, deep)), dma((chunks, deep)),
         dma((chunks, deep)), dma((chunks, deep)), dma((chunks,)), dma((chunks,)), dma((rows,)), dma((rows,)),
     ]

time: 187 us -> 175 us (0.936)
  Pallas kernels: 182 us -> 171 us
    pallas_call x1, Pallas kernels: 182 us -> 171 us  [fused_layer(): pl.pallas_call(functools.partial(layer_kernel, (rows, cols, tokens, width...]
where the time goes in v2:
time: 175 us
  Pallas kernels  171 us (98%)
  local copies, waits for them, and re-layouts  4.22 us (2%)
    pallas_call x1, Pallas kernels, fused_layer(): pl.pallas_call(functools.partial(layer_kernel, (rows, cols, tokens, width...  171 us

profile of v2, /device:TPU:0, one launch (start us, length us, event | category | flops | bytes accessed | tf_op | source)
XLA Modules:
  0.0 175.1 jit_solution(561609720499628936)
XLA Ops:
  0.0 1.3 reshape.6.gain_a
  1.3 1.3 reshape.7.gain_f
  2.6 170.9 %shard_map.109 = bf16[16,8192]{1,0:T(8,128)(2,1)} custom-call(bf16[16,8192]{1,0:T(8,128)(2,1)} %chars.1, bf16[8192,1024]{1,0:T(8,128)(2,1)} %pool_w.1, bf16[1,1024]{1,0:T(2,128)(2,1)} %reshape.6.gain_a, bf16[1024,2048]{1,0:T(8,128)(2,1)} %wq.1, bf16[1024,2048]{1,0:T(8,128)(2,1)} %wk.1, bf16[1024,2048]{1,0:T(8,128)(2,1)} %wv.1, bf16[2048,1024]{1,0:T(8,128)(2,1)} %wo.1, ...), custom_call_target="tpu_custom_call" | custom-call | tf_op jit(solution)/shard_map/pallas_call | solution.py:612
  173.4 1.7 copy.13
